TPU v7x, 32 devices: a whole 2x2x4 slice. The times are simulated.
32 devices in a mesh: dp: 2 (over x), ctx: 8 (over z, core), tp: 2 (over y).
Axes of the slice: x: 2, y: 2, z: 4, core: 2. Of those that a mesh axis runs over, the one named last changes fastest.
Arguments:
- query: bfloat16 [2048, 12288], P(('dp', 'ctx'), 'tp'), parts along dimension 0
- keys: bfloat16 [2048, 1024], P(('dp', 'ctx'), 'tp'), parts along dimension 0
- values: bfloat16 [2048, 1024], P(('dp', 'ctx'), 'tp'), parts along dimension 0, may hold values from -6 to 6
- doc_lengths: int32 [32], P('dp'), parts along dimension 0, may hold values from 1 to 640, 1024 in all
- gain: bfloat16 [12288], P('tp'), may hold values from 0.5 to 1.5
Outputs:
- normed: bfloat16 [2048, 12288], P(('dp', 'ctx'), 'tp'), parts along dimension 0
There are 2 independent parts, one for each index of `dp`. A program takes and returns all parts, laid end to end along the dimension named above; an argument that names none is the same for every part. Nothing has to cross between parts.
Inputs may be any that keep to these rules, and one draw needn't show every extreme that they name: `doc_lengths`: the lengths sum to 1024; the longest is exactly 640.
All inputs are finite; a program needn't handle non-finite values.
Results may differ from a plain program's by a relative error of at most 0.015.
Values may be sent and summed in bfloat16 or wider, within the bound.
A program may use at most 64 MiB of HBM per device.

v0:
```python
import jax
import jax.numpy as jnp
from jax import lax
from jax.sharding import PartitionSpec as P

QUERY_HEADS = 96
HEAD_SIZE = 128


def body(query, keys, values, doc_lengths, gain):
    rows = query.shape[0]
    heads_local = query.shape[1] // HEAD_SIZE
    groups = keys.shape[1] // HEAD_SIZE
    query_group_ratio = heads_local // groups
    scale = HEAD_SIZE ** (-0.5)
    ends = jnp.cumsum(doc_lengths)

    def doc_index(positions):
        return jnp.sum((positions[:, None] >= ends[None, :]).astype(jnp.int32), axis=1)

    q_start = lax.axis_index("ctx") * rows
    q_pos = q_start + jnp.arange(rows, dtype=jnp.int32)
    q_doc = doc_index(q_pos)
    q_four = query.reshape(rows, groups, query_group_ratio, HEAD_SIZE)

    def attend(state, k_piece, v_piece, k_start):
        count = k_piece.shape[0]
        k_pos = k_start + jnp.arange(count, dtype=jnp.int32)
        k_doc = doc_index(k_pos)
        allowed = (
            (k_doc[None, :] == q_doc[:, None])
            & (k_pos[None, :] <= q_pos[:, None])
            & (k_pos[None, :] >= 0)
        )
        scores = (
            jnp.einsum(
                "sgrd,ngd->grsn",
                q_four,
                k_piece.reshape(count, groups, HEAD_SIZE),
                preferred_element_type=jnp.float32,
            )
            * scale
        )
        scores = jnp.where(allowed, scores, -1e30)
        top_old, total_old, acc_old = state
        top_new = jnp.maximum(top_old, jnp.max(scores, axis=-1))
        probs = jnp.where(allowed, jnp.exp(scores - top_new[..., None]), 0.0)
        correct = jnp.exp(top_old - top_new)
        total_new = total_old * correct + jnp.sum(probs, axis=-1)
        update = jnp.einsum(
            "grsn,ngd->grsd",
            probs.astype(jnp.bfloat16),
            v_piece.reshape(count, groups, HEAD_SIZE),
            preferred_element_type=jnp.float32,
        )
        return (top_new, total_new, acc_old * correct[..., None] + update)

    start_state = (
        jnp.full((groups, query_group_ratio, rows), -1e30, jnp.float32),
        jnp.zeros((groups, query_group_ratio, rows), jnp.float32),
        jnp.zeros((groups, query_group_ratio, rows, HEAD_SIZE), jnp.float32),
    )
    k_piece = lax.all_gather(keys, "ctx", axis=0, tiled=True)
    v_piece = lax.all_gather(values, "ctx", axis=0, tiled=True)
    count = k_piece.shape[0]
    block = 512

    def one_block(i, inner):
        k_block = lax.dynamic_slice_in_dim(k_piece, i * block, block, 0)
        v_block = lax.dynamic_slice_in_dim(v_piece, i * block, block, 0)
        return attend(inner, k_block, v_block, i * block)

    top, total, acc = lax.fori_loop(0, count // block, one_block, start_state)
    context = (
        jnp.transpose(acc / total[..., None], (2, 0, 1, 3))
        .reshape(rows, heads_local * HEAD_SIZE)
        .astype(jnp.bfloat16)
    )
    wide = context.astype(jnp.float32)
    squares_sum = lax.psum(jnp.sum(wide * wide, axis=1), "tp")
    power = squares_sum / (QUERY_HEADS * HEAD_SIZE)
    return (wide * gain.astype(jnp.float32)[None, :] / jnp.sqrt(power + 1e-06)[:, None]).astype(
        jnp.bfloat16
    )


def solution(mesh):
    return jax.shard_map(
        body,
        mesh=mesh,
        in_specs=(
            P(("dp", "ctx"), "tp"),
            P(("dp", "ctx"), "tp"),
            P(("dp", "ctx"), "tp"),
            P("dp"),
            P("tp"),
        ),
        out_specs=P(("dp", "ctx"), "tp"),
        check_vma=False,
    )
```

profile of v0, /device:TPU:0, one launch (start us, length us, event | category | flops | bytes accessed | tf_op | source)
XLA Modules:
  0.0 128.3 jit_solution(3450541017377578037)
XLA Ops:
  6.5 1.7 %copy.23 = bf16[128,512]{0,1:T(8,128)(2,1)} copy(bf16[128,512]{1,0:T(8,128)(2,1)} %param.8) | data formatting | bytes 262144 | tf_op args[1]
  8.3 1.6 %copy.25 = bf16[128,512]{0,1:T(8,128)(2,1)} copy(bf16[128,512]{1,0:T(8,128)(2,1)} %param.9) | data formatting | bytes 262144 | tf_op args[2]
  10.0 0.7 copy.22
  10.9 1.9 %copy.24 = bf16[128,6144]{0,1:T(8,128)(2,1)S(1)} copy(bf16[128,6144]{1,0:T(8,128)(2,1)} %param.7) | data formatting | bytes 3145728 | tf_op args[0]
  12.8 0.9 copy.26
  13.8 21.8 %all-gather.3.cloned.1.call-done = bf16[1024,512]{0,1:T(8,128)(2,1)} async-done(((bf16[128,512]{0,1:T(8,128)(2,1)}), bf16[1024,512]{0,1:T(8,128)(2,1)}) %all-gather.3.cloned.1.call-update) | async-done | bytes 1048592 | tf_op jit(solution)/shard_map/all_gather | solution.py:63
  35.7 24.2 %all-gather.5.cloned.1.call-done = bf16[1024,512]{0,1:T(8,128)(2,1)} async-done(((bf16[128,512]{0,1:T(8,128)(2,1)}), bf16[1024,512]{0,1:T(8,128)(2,1)}) %all-gather.5.cloned.1.call-update) | async-done | bytes 1048592 | tf_op jit(solution)/shard_map/all_gather | solution.py:64
  59.9 45.9 %while.18 = (s32[]{:T(128)}, f32[4,12,128]{2,1,0:T(8,128)S(1)}, f32[4,12,128]{2,1,0:T(8,128)S(1)}, f32[4,12,128,128]{3,2,1,0:T(8,128)}, s32[16]{0:T(128)S(1)}, /...) while((s32[]{:T(128)}, f32[4,12,128]{2,1,0:T(8,128)S(1)}, ...), condition=%wide.region_6.7_spmd.clone, body=%wide.region_2.6_spmd.clone.sunk | while | flops 1654185088 | bytes 99758888 | solution.py:73
  60.0 0.3 and_and_fusion.2
  60.2 1.3 constant_dynamic-slice_fusion.3
  61.5 6.6 %fusion.34 = (f32[4,12,128]{2,1,0:T(8,128)S(1)}, f32[4,512,128,12]{2,1,3,0:T(8,128)}) fusion(pred[128,512]{0,1:T(8,128)(4,1)S(1)} %and_and_fusion.2, bf16[512,4,128,1]{0,2,3,1:T(8,128)(2,1)S(1)} %bitcast.52, bf16[128,4,12,128]{3,0,2,1:T(8,128)(2,1)S(1)} %get-tuple-element.369), kind=kOutput, calls=%fused_computation.3.clone.1 | convolution fusion | flops 814737408 | bytes 14770176 | tf_op jit(solution)/shard_map/while/body/eval_jaxpr/sgrd,ngd->grsn/dot_general | solution.py:36
  68.1 6.8 %fusion.35 = f32[4,12,128]{2,1,0:T(8,128)S(1)} fusion(f32[4,512,128,12]{2,1,3,0:T(8,128)} %get-tuple-element.330, f32[4,12,128]{2,1,0:T(8,128)S(1)} %select_maximum_fusion.2, pred[128,512]{0,1:T(8,128)(4,1)S(1)} %and_and_fusion.2), kind=kLoop, calls=%fused_computation.5.clone.1 | loop fusion | flops 15722496 | bytes 12697600 | tf_op jit(solution)/shard_map/while/body/eval_jaxpr/reduce_sum | solution.py:49
  75.0 1.4 %copy-done = f32[4,512,128,12]{2,1,3,0:T(8,128)S(1)} copy-done((f32[4,512,128,12]{2,1,3,0:T(8,128)S(1)}, f32[4,512,128,12]{2,1,3,0:T(8,128)}, u32[]{:S(2)}) %copy-start) | copy-done | bytes 12582936 | tf_op jit(solution)/shard_map/while
  76.4 5.8 %fusion.37 = f32[4,12,128,128]{3,2,1,0:T(8,128)} fusion(f32[4,12,128,128]{3,2,1,0:T(8,128)} %get-tuple-element.351, bf16[512,4,128,1]{0,2,3,1:T(8,128)(2,1)S(1)} %bitcast.53, f32[4,512,128,12]{2,1,3,0:T(8,128)S(1)} %copy-done, f32[4,12,128]{2,1,0:T(8,128)S(1)} %select_maximum_fusion.2, pred[128,512]{0,1:T(8,128)(4,1)S(1)} %and_and_fusion.2, ...), kind=kOutput, calls=%fused_computation.9.clone.1 | convolution fusion | flops 823394304 | bytes 19513344 | tf_op jit(solution)/shard_map/while/body/eval_jaxpr/grsn,ngd->grsd/dot_general | solution.py:50
  82.5 1.3 constant_dynamic-slice_fusion.3
  83.8 6.6 %fusion.34 = (f32[4,12,128]{2,1,0:T(8,128)S(1)}, f32[4,512,128,12]{2,1,3,0:T(8,128)}) fusion(pred[128,512]{0,1:T(8,128)(4,1)S(1)} %and_and_fusion.2, bf16[512,4,128,1]{0,2,3,1:T(8,128)(2,1)S(1)} %bitcast.52, bf16[128,4,12,128]{3,0,2,1:T(8,128)(2,1)S(1)} %get-tuple-element.369), kind=kOutput, calls=%fused_computation.3.clone.1 | convolution fusion | flops 814737408 | bytes 14770176 | tf_op jit(solution)/shard_map/while/body/eval_jaxpr/sgrd,ngd->grsn/dot_general | solution.py:36
  90.4 6.8 %fusion.35 = f32[4,12,128]{2,1,0:T(8,128)S(1)} fusion(f32[4,512,128,12]{2,1,3,0:T(8,128)} %get-tuple-element.330, f32[4,12,128]{2,1,0:T(8,128)S(1)} %select_maximum_fusion.2, pred[128,512]{0,1:T(8,128)(4,1)S(1)} %and_and_fusion.2), kind=kLoop, calls=%fused_computation.5.clone.1 | loop fusion | flops 15722496 | bytes 12697600 | tf_op jit(solution)/shard_map/while/body/eval_jaxpr/reduce_sum | solution.py:49
  97.3 1.4 %copy-done = f32[4,512,128,12]{2,1,3,0:T(8,128)S(1)} copy-done((f32[4,512,128,12]{2,1,3,0:T(8,128)S(1)}, f32[4,512,128,12]{2,1,3,0:T(8,128)}, u32[]{:S(2)}) %copy-start) | copy-done | bytes 12582936 | tf_op jit(solution)/shard_map/while
  98.7 7.1 %fusion.37 = f32[4,12,128,128]{3,2,1,0:T(8,128)} fusion(f32[4,12,128,128]{3,2,1,0:T(8,128)} %get-tuple-element.351, bf16[512,4,128,1]{0,2,3,1:T(8,128)(2,1)S(1)} %bitcast.53, f32[4,512,128,12]{2,1,3,0:T(8,128)S(1)} %copy-done, f32[4,12,128]{2,1,0:T(8,128)S(1)} %select_maximum_fusion.2, pred[128,512]{0,1:T(8,128)(4,1)S(1)} %and_and_fusion.2, ...), kind=kOutput, calls=%fused_computation.9.clone.1 | convolution fusion | flops 823394304 | bytes 19513344 | tf_op jit(solution)/shard_map/while/body/eval_jaxpr/grsn,ngd->grsd/dot_general | solution.py:50
  105.8 3.5 %copy.27 = f32[4,12,128,128]{2,3,1,0:T(8,128)} copy(f32[4,12,128,128]{3,2,1,0:T(8,128)} %get-tuple-element.175) | data formatting | bytes 6291456 | tf_op jit(solution)/shard_map/while | solution.py:73
  109.3 2.7 %multiply_reduce_fusion = (f32[128]{0:T(128)S(1)}, f32[4,12,128,128]{2,3,1,0:T(8,128)S(1)}) fusion(f32[4,12,128,128]{2,3,1,0:T(8,128)} %copy.27, f32[4,12,128]{2,1,0:T(8,128)S(1)} %get-tuple-element.176), kind=kLoop, calls=%fused_computation.27 | loop fusion | flops 3932032 | bytes 6316544 | tf_op jit(solution)/shard_map/reduce_sum | solution.py:80
  112.1 4.9 %psum.7 = f32[128]{0:T(128)S(1)} all-reduce(f32[128]{0:T(128)S(1)} %get-tuple-element.255), channel_id=1, replica_groups=mesh['dp'=2,'ctx'=8,'tp'=2] {'tp'}, use_global_device_ids=true, to_apply=%region_8.9 | all-reduce | flops 128 | bytes 1024 | tf_op jit(solution)/shard_map/psum | solution.py:80
  117.0 1.9 %fusion.16 = bf16[128,6144]{0,1:T(8,128)(2,1)} fusion(f32[4,12,128,128]{2,3,1,0:T(8,128)S(1)} %get-tuple-element.256, f32[128]{0:T(128)S(1)} %add_sqrt_fusion, f32[6144]{0:T(1024)S(1)} %convert_element_type.48), kind=kLoop, calls=%fused_computation.26 | loop fusion | flops 2359296 | bytes 4743680 | tf_op jit(solution)/shard_map/convert_element_type | solution.py:82
  118.9 2.6 %copy.28 = bf16[128,6144]{1,0:T(8,128)(2,1)} copy(bf16[128,6144]{0,1:T(8,128)(2,1)} %fusion.16) | data formatting | bytes 3145728 | tf_op jit(solution)/shard_map/convert_element_type | solution.py:82
  (32 shorter events, 0.9 us)
Async XLA Ops:
  6.5 29.1 %all-gather.3.cloned.1.call-start = ((), (), s32[]{:S(2)}) async-start(), calls=%async_computation | async-start | bytes 1179648 | tf_op jit(solution)/shard_map/all_gather | solution.py:63
  8.2 51.6 %all-gather.5.cloned.1.call-start = ((), (), s32[]{:S(2)}) async-start(), calls=%async_computation.1 | async-start | bytes 1179648 | tf_op jit(solution)/shard_map/all_gather | solution.py:64
  10.9 2.8 %copy-start.1 = (bf16[6144]{0:T(1024)(128)(2,1)S(1)}, bf16[6144]{0:T(1024)(128)(2,1)}, u32[]{:S(2)}) copy-start(bf16[6144]{0:T(1024)(128)(2,1)} %param.11) | copy-start | bytes 36868
  68.1 8.2 %copy-start = (f32[4,512,128,12]{2,1,3,0:T(8,128)S(1)}, f32[4,512,128,12]{2,1,3,0:T(8,128)}, u32[]{:S(2)}) copy-start(f32[4,512,128,12]{2,1,3,0:T(8,128)} %get-tuple-element.330) | copy-start | bytes 37748740 | tf_op jit(solution)/shard_map/while
  90.4 8.2 %copy-start = (f32[4,512,128,12]{2,1,3,0:T(8,128)S(1)}, f32[4,512,128,12]{2,1,3,0:T(8,128)}, u32[]{:S(2)}) copy-start(f32[4,512,128,12]{2,1,3,0:T(8,128)} %get-tuple-element.330) | copy-start | bytes 37748740 | tf_op jit(solution)/shard_map/while
Sparse Core Ops, SparseCore 0:
  8.9 26.6 all-gather.2
  37.2 22.5 all-gather.4
where the time goes:
time: 129 us; the launch traced here: 128 us
  waiting for transfers between devices  46.1 us (36%)
  matrix products  26.1 us (20%)
  other arithmetic  19.3 us (15%)
  local copies, waits for them, and re-layouts  18.3 us (14%)
  between operations  13.5 us (10%)
  blocking collectives  4.94 us (4%)
    all_gather x1, waiting for transfers between devices, body(): v_piece = lax.all_gather(values, 'ctx', axis=0, tiled=True)  24.2 us
    all_gather x1, waiting for transfers between devices, body(): k_piece = lax.all_gather(keys, 'ctx', axis=0, tiled=True)  21.8 us
    reduce_sum x2, other arithmetic, attend(): total_new = total_old * correct + jnp.sum(probs, axis=-1)  13.6 us
    dot_general x2, matrix products, attend(): jnp.einsum('sgrd,ngd->grsn', q_four, k_piece.reshape(count, groups, HEAD_...  13.2 us
    dot_general x2, matrix products, attend(): jnp.einsum('grsn,ngd->grsd', probs.astype(jnp.bfloat16), v_piece.reshape(...  12.9 us
    unnamed x6, local copies, waits for them, and re-layouts  6.13 us
    psum x1, blocking collectives, body(): squares_sum = lax.psum(jnp.sum(wide * wide, axis=1), 'tp')  4.94 us
    while x1, local copies, waits for them, and re-layouts, body(): top, total, acc = lax.fori_loop(0, count // block, one_block, start_state)  3.55 us
  transfers between devices with their start and end apart: 2, of which 2 were waited for; matrix products, arithmetic and copies ran while one was open for 4% of the time, Pallas kernels for 0%

commit v1 on v0

v1 whole, which is shorter than its diff:
```python
import functools
import math

import jax
import jax.numpy as jnp
from jax import lax
from jax.experimental import pallas as pl
from jax.experimental.pallas import tpu as pltpu
from jax.sharding import PartitionSpec as P

QUERY_HEADS = 96
HEAD_SIZE = 128
LOW = -1e31
MESH = pl.DeviceIdType.MESH
UNIT = 2


def attention_kernel(
    ctx_size, tp_size, back, ratio,
    query_ref, keys_ref, values_ref, lengths_ref,
    context_ref, inverse_ref,
    kv, q_v, out_v, lengths, cap, top, acc, squares, sums, sums_in,
    kv_sem, q_sem, len_sem, out_sem,
    recv_sem, fwd_sem, relay_sem, tp_send, tp_recv,
):
    rows = query_ref.shape[0]
    groups = keys_ref.shape[1] // HEAD_SIZE
    wide = ratio * HEAD_SIZE
    pairs = back // 2 + 1
    docs = lengths.shape[0]
    chips = ctx_size // 2
    me = lax.axis_index("ctx")
    my_tp = lax.axis_index("tp")
    chip = me // 2
    core = me % 2
    has_next = (chip + 1 < chips).astype(jnp.int32)
    factor = HEAD_SIZE ** (-0.5) * math.log2(math.e)

    def columns(g, width):
        return pl.ds(pl.multiple_of(g * width, width), width)

    def own_kv(g, which):
        src = (keys_ref, values_ref)[which]
        return pltpu.make_async_copy(
            src.at[:, columns(g, HEAD_SIZE)], kv.at[0, g, which], kv_sem.at[which, g]
        )

    def own_q(g):
        return pltpu.make_async_copy(query_ref.at[:, columns(g, wide)], q_v.at[g], q_sem.at[g])

    def write_out(g):
        return pltpu.make_async_copy(out_v.at[g], context_ref.at[:, columns(g, wide)], out_sem.at[g])

    own_lengths = pltpu.make_async_copy(lengths_ref, lengths, len_sem)

    for g in range(groups):
        own_kv(g, 0).start()
        own_kv(g, 1).start()
    own_lengths.start()
    for g in range(groups):
        own_q(g).start()

    barrier = pltpu.get_barrier_semaphore()

    def greet(ctx):
        pl.semaphore_signal(barrier, inc=1, device_id={"ctx": ctx}, device_id_type=MESH)

    greet(me + 1 - 2 * core)

    @pl.when(has_next == 1)
    def _():
        greet(me + 2)

    @pl.when(chip > 0)
    def _():
        greet(me - 2)

    @pl.when(core * has_next == 1)
    def _():
        greet(me + 1)

    @pl.when((1 - core) * chip > 0)
    def _():
        greet(me - 1)

    for o in range(1, tp_size):
        pl.semaphore_signal(
            barrier, inc=1, device_id={"tp": lax.rem(my_tp + o, tp_size)}, device_id_type=MESH
        )

    for d in range(1, 2 * pairs):
        def clear():
            kv[d] = jnp.zeros_like(kv[d])
        if d > back:
            clear()
        else:
            pl.when(me < d)(clear)

    own_lengths.wait()
    position = me * rows + lax.broadcasted_iota(jnp.int32, (rows, rows), 0)
    lane = lax.broadcasted_iota(jnp.int32, (rows, rows), 1)
    first = jnp.zeros((rows, rows), jnp.int32)
    end = jnp.int32(0)
    for i in range(docs):
        end = end + lengths[i]
        first = jnp.where(position >= end, end, first)
    for d in range(2 * pairs):
        key = (me - d) * rows + lane
        allowed = (key >= first) & (key <= position)
        cap[d // 2, :, (d % 2) * rows:(d % 2 + 1) * rows] = jnp.where(
            allowed, jnp.float32(jnp.inf), jnp.float32(LOW)
        )

    has_last = jnp.minimum(chip, 1)
    greeted = tp_size + has_next + has_last + core * has_next + (1 - core) * has_last
    pl.semaphore_wait(barrier, greeted)

    def send(src_slot, dst_slot, g, send_sem, ctx):
        return pltpu.make_async_remote_copy(
            src_ref=kv.at[src_slot, g],
            dst_ref=kv.at[dst_slot, g],
            send_sem=send_sem.at[src_slot // 2, g],
            recv_sem=recv_sem.at[dst_slot, g],
            device_id={"ctx": ctx},
            device_id_type=MESH,
        )

    def arrived(d, g):
        send(0, d, g, fwd_sem, me + 1 - 2 * core).wait_recv()

    def sends(e, g, act):
        if e + 2 <= back:
            @pl.when(has_next == 1)
            def _():
                act(send(e, e + 2, g, fwd_sem, me + 2))
        elif e + 1 <= back:
            @pl.when(core * has_next == 1)
            def _():
                act(send(e, e + 1, g, fwd_sem, me + 1))
        relay = send(e, e + 1 - 2 * core, g, relay_sem, me + 1 - 2 * core)
        if e == 0:
            pl.when(core == 0)(lambda: act(relay))
        elif e + 1 <= back:
            act(relay)
        else:
            pl.when(core == 1)(lambda: act(relay))

    def start(copy):
        copy.start()

    def finish(copy):
        copy.wait_send()

    def pass_on(g, carry):
        own_kv(g, 0).wait()
        own_kv(g, 1).wait()
        sends(0, g, start)
        return carry

    lax.fori_loop(0, groups, pass_on, 0)

    squares[...] = jnp.zeros_like(squares)

    def attend(j, g):
        k = jnp.concatenate([kv[2 * j, g, 0], kv[2 * j + 1, g, 0]], axis=0)
        v = jnp.concatenate([kv[2 * j, g, 1], kv[2 * j + 1, g, 1]], axis=0)
        v = jnp.concatenate([v, jnp.ones_like(v)], axis=1)
        for u in range(0, ratio, UNIT):
            heads = range(u, u + UNIT)
            q = jnp.concatenate(
                [q_v[g, :, h * HEAD_SIZE:(h + 1) * HEAD_SIZE] for h in heads], axis=0
            )
            s = lax.dot_general(
                q, k, (((1,), (1,)), ((), ())), preferred_element_type=jnp.float32
            )
            probs, tops, olds = [], [], []
            for n, h in enumerate(heads):
                part = jnp.minimum(s[n * rows:(n + 1) * rows], cap[j])
                high = jnp.broadcast_to(
                    jnp.max(part, axis=1, keepdims=True), (rows, HEAD_SIZE)
                )
                if j > 0:
                    old = top[g * ratio + h]
                    high = jnp.maximum(old, high)
                    olds.append(old)
                tops.append(high)
                both = jnp.concatenate([high, high], axis=1)
                probs.append(jnp.exp2((part - both) * factor).astype(jnp.bfloat16))
            update = jnp.dot(
                jnp.concatenate(probs, axis=0), v, preferred_element_type=jnp.float32
            )
            for n, h in enumerate(heads):
                at = g * ratio + h
                a = update[n * rows:(n + 1) * rows, :HEAD_SIZE]
                t = update[n * rows:(n + 1) * rows, HEAD_SIZE:]
                if j > 0:
                    correct = jnp.exp2((olds[n] - tops[n]) * factor)
                    a = a + acc[at, :, :HEAD_SIZE] * correct
                    t = t + acc[at, :, HEAD_SIZE:] * correct
                if j < pairs - 1:
                    top[at] = tops[n]
                    acc[at, :, :HEAD_SIZE] = a
                    acc[at, :, HEAD_SIZE:] = t
                else:
                    c = (a / t).astype(jnp.bfloat16)
                    out_v[g, :, h * HEAD_SIZE:(h + 1) * HEAD_SIZE] = c
                    c = c.astype(jnp.float32)
                    squares[...] += c * c

    for j in range(pairs):
        def step(g, carry):
            even, odd = 2 * j + 2, 2 * j + 1
            if even <= back:
                @pl.when(me >= even)
                def _():
                    arrived(even, g)
                    sends(even, g, start)
            if odd <= back:
                @pl.when(me >= odd)
                def _():
                    arrived(odd, g)
            if j == 0:
                own_q(g).wait()
            attend(j, g)
            if j == pairs - 1:
                write_out(g).start()
            return carry

        lax.fori_loop(0, groups, step, 0)

    mine = jnp.sum(squares[...].T, axis=0, keepdims=True)
    sums[...] = jnp.broadcast_to(mine, sums.shape)
    copies = []
    for o in range(1, tp_size):
        copies.append(pltpu.make_async_remote_copy(
            src_ref=sums,
            dst_ref=sums_in.at[o - 1],
            send_sem=tp_send.at[o - 1],
            recv_sem=tp_recv.at[o - 1],
            device_id={"tp": lax.rem(my_tp + o, tp_size)},
            device_id_type=MESH,
        ))
        copies[-1].start()

    def drain(g, carry):
        for e in range(0, back + 1, 2):
            if e == 0:
                sends(e, g, finish)
            else:
                pl.when(me >= e)(lambda: sends(e, g, finish))
        write_out(g).wait()
        return carry

    lax.fori_loop(0, groups, drain, 0)
    total = mine
    for o, copy in enumerate(copies):
        copy.wait()
        total = total + sums_in[o, 0:1, :]
    power = total / (QUERY_HEADS * HEAD_SIZE)
    inverse = 1.0 / jnp.sqrt(power + 1e-06)
    inverse_ref[...] = jnp.broadcast_to(inverse, (rows, rows)).T


def body(ctx_size, tp_size, query, keys, values, doc_lengths, gain):
    rows = query.shape[0]
    groups = keys.shape[1] // HEAD_SIZE
    heads = query.shape[1] // HEAD_SIZE
    ratio = heads // groups
    longest = rows * ctx_size * 5 // 8
    back = min(-(-(longest - 1) // rows), ctx_size - 1)
    pairs = back // 2 + 1
    context, inverse = pl.pallas_call(
        functools.partial(attention_kernel, ctx_size, tp_size, back, ratio),
        out_shape=(
            jax.ShapeDtypeStruct(query.shape, jnp.bfloat16),
            jax.ShapeDtypeStruct((rows, rows), jnp.float32),
        ),
        in_specs=[pl.BlockSpec(memory_space=pltpu.HBM)] * 4,
        out_specs=(
            pl.BlockSpec(memory_space=pl.ANY),
            pl.BlockSpec(memory_space=pltpu.VMEM),
        ),
        scratch_shapes=[
            pltpu.VMEM((2 * pairs, groups, 2, rows, HEAD_SIZE), jnp.bfloat16),
            pltpu.VMEM((groups, rows, ratio * HEAD_SIZE), jnp.bfloat16),
            pltpu.VMEM((groups, rows, ratio * HEAD_SIZE), jnp.bfloat16),
            pltpu.SMEM(doc_lengths.shape, jnp.int32),
            pltpu.VMEM((pairs, rows, 2 * rows), jnp.float32),
            pltpu.VMEM((heads, rows, HEAD_SIZE), jnp.float32),
            pltpu.VMEM((heads, rows, 2 * HEAD_SIZE), jnp.float32),
            pltpu.VMEM((rows, HEAD_SIZE), jnp.float32),
            pltpu.VMEM((8, rows), jnp.float32),
            pltpu.VMEM((tp_size, 8, rows), jnp.float32),
            pltpu.SemaphoreType.DMA((2, groups)),
            pltpu.SemaphoreType.DMA((groups,)),
            pltpu.SemaphoreType.DMA,
            pltpu.SemaphoreType.DMA((groups,)),
            pltpu.SemaphoreType.DMA((2 * pairs, groups)),
            pltpu.SemaphoreType.DMA((pairs, groups)),
            pltpu.SemaphoreType.DMA((pairs, groups)),
            pltpu.SemaphoreType.DMA((tp_size,)),
            pltpu.SemaphoreType.DMA((tp_size,)),
        ],
        compiler_params=pltpu.CompilerParams(
            collective_id=0, has_side_effects=True, vmem_limit_bytes=40 * 2**20
        ),
        cost_estimate=pl.CostEstimate(
            flops=4 * heads * rows * 2 * pairs * rows * HEAD_SIZE,
            bytes_accessed=4 * query.size + 4 * keys.size,
            transcendentals=heads * rows * 2 * pairs * rows,
        ),
    )(query, keys, values, doc_lengths)
    return (
        context.astype(jnp.float32) * gain.astype(jnp.float32)[None, :] * inverse[:, :1]
    ).astype(jnp.bfloat16)


def solution(mesh):
    return jax.shard_map(
        functools.partial(body, mesh.shape["ctx"], mesh.shape["tp"]),
        mesh=mesh,
        in_specs=(
            P(("dp", "ctx"), "tp"),
            P(("dp", "ctx"), "tp"),
            P(("dp", "ctx"), "tp"),
            P("dp"),
            P("tp"),
        ),
        out_specs=P(("dp", "ctx"), "tp"),
        check_vma=False,
    )
```

time: 129 us -> 30 us (0.23)
  the two profiles are of different devices: /device:TPU:0 before, /device:TPU:24 now
where the time goes in v1:
time: 30 us; the launch traced here: 29.8 us
  Pallas kernels  23.5 us (78%)
  local copies, waits for them, and re-layouts  3.97 us (13%)
  other arithmetic  2.28 us (8%)
    pallas_call x1, Pallas kernels, body(): pl.pallas_call(functools.partial(attention_kernel, ctx_size, tp_size, bac...  23.5 us
    unnamed x8, local copies, waits for them, and re-layouts  3.87 us
    convert_element_type x1, other arithmetic, body(): return (context.astype(jnp.float32) * gain.astype(jnp.float32)[None, :] *...  1.57 us
    convert_element_type x1, other arithmetic, body(): gain.astype(jnp.float32)[None, :]  0.71 us

profile of v1, /device:TPU:24, one launch (start us, length us, event | category | flops | bytes accessed | tf_op | source)
XLA Modules:
  0.0 29.8 jit_solution(14257942896939473291)
XLA Ops:
  0.0 0.7 %convert_element_type.10 = f32[6144]{0:T(1024)S(1)} convert(bf16[6144]{0:T(1024)(128)(2,1)} %param.9) | non-fusion elementwise | flops 6144 | bytes 36864 | tf_op jit(solution)/shard_map/convert_element_type | solution.py:314
  0.7 0.0 copy-start
  0.7 1.4 %copy-done = bf16[128,6144]{1,0:T(8,128)(2,1)S(1)} copy-done((bf16[128,6144]{1,0:T(8,128)(2,1)S(1)}, bf16[128,6144]{1,0:T(8,128)(2,1)}, u32[]{:S(2)}) %copy-start) | copy-done | bytes 1572888
  2.1 0.0 copy-start.1
  2.1 0.9 %copy-done.1 = bf16[128,512]{1,0:T(8,128)(2,1)S(1)} copy-done((bf16[128,512]{1,0:T(8,128)(2,1)S(1)}, bf16[128,512]{1,0:T(8,128)(2,1)}, u32[]{:S(2)}) %copy-start.1) | copy-done | bytes 131096
  3.0 0.0 copy-start.2
  3.0 0.9 %copy-done.2 = bf16[128,512]{1,0:T(8,128)(2,1)S(1)} copy-done((bf16[128,512]{1,0:T(8,128)(2,1)S(1)}, bf16[128,512]{1,0:T(8,128)(2,1)}, u32[]{:S(2)}) %copy-start.2) | copy-done | bytes 131096
  3.9 0.0 copy-start.3
  3.9 0.7 %copy-done.3 = s32[16]{0:T(128)S(1)} copy-done((s32[16]{0:T(128)S(1)}, s32[16]{0:T(128)}, u32[]{:S(2)}) %copy-start.3) | copy-done | bytes 88
  4.6 23.5 %shard_map.55 = (bf16[128,6144]{1,0:T(8,128)(2,1)S(1)}, f32[128,128]{1,0:T(8,128)S(1)}) custom-call(bf16[128,6144]{1,0:T(8,128)(2,1)S(1)} %copy-done, bf16[128,512]{1,0:T(8,128)(2,1)S(1)} %copy-done.1, bf16[128,512]{1,0:T(8,128)(2,1)S(1)} %copy-done.2, s32[16]{0:T(128)S(1)} %copy-done.3), custom_call_target="tpu_custom_call" | custom-call | flops 2415919104 | bytes 3407872 | tf_op jit(solution)/shard_map/pallas_call | solution.py:272
  28.1 0.1 slice_reduce_fusion
  28.2 1.6 %multiply_convert_fusion = bf16[128,6144]{1,0:T(8,128)(2,1)} fusion(bf16[128,6144]{1,0:T(8,128)(2,1)S(1)} %get-tuple-element.7, f32[128]{0:T(128)S(1)} %slice_reduce_fusion, f32[6144]{0:T(1024)S(1)} %convert_element_type.10), kind=kLoop, calls=%fused_computation | loop fusion | flops 3145728 | bytes 3170816 | tf_op jit(solution)/shard_map/convert_element_type | solution.py:315
Async XLA Ops:
  0.7 1.4 %copy-start = (bf16[128,6144]{1,0:T(8,128)(2,1)S(1)}, bf16[128,6144]{1,0:T(8,128)(2,1)}, u32[]{:S(2)}) copy-start(bf16[128,6144]{1,0:T(8,128)(2,1)} %query_ref.1) | copy-start | bytes 4718596
  2.1 0.9 %copy-start.1 = (bf16[128,512]{1,0:T(8,128)(2,1)S(1)}, bf16[128,512]{1,0:T(8,128)(2,1)}, u32[]{:S(2)}) copy-start(bf16[128,512]{1,0:T(8,128)(2,1)} %keys_ref.1) | copy-start | bytes 393220
  3.0 0.9 %copy-start.2 = (bf16[128,512]{1,0:T(8,128)(2,1)S(1)}, bf16[128,512]{1,0:T(8,128)(2,1)}, u32[]{:S(2)}) copy-start(bf16[128,512]{1,0:T(8,128)(2,1)} %values_ref.1) | copy-start | bytes 393220
  3.9 0.7 %copy-start.3 = (s32[16]{0:T(128)S(1)}, s32[16]{0:T(128)}, u32[]{:S(2)}) copy-start(s32[16]{0:T(128)} %lengths_ref.1) | copy-start | bytes 196

commit v2 on v1

--- a/solution.py
+++ b/solution.py
@@ -12,15 +12,15 @@
 HEAD_SIZE = 128
 LOW = -1e31
 MESH = pl.DeviceIdType.MESH
-UNIT = 2
+UNIT = 4
 
 
 def attention_kernel(
     ctx_size, tp_size, back, ratio,
-    query_ref, keys_ref, values_ref, lengths_ref,
-    context_ref, inverse_ref,
-    kv, q_v, out_v, lengths, cap, top, acc, squares, sums, sums_in,
-    kv_sem, q_sem, len_sem, out_sem,
+    query_ref, keys_ref, values_ref, lengths_ref, gain_ref,
+    context_ref, inverse_ref, wide_gain_ref,
+    kv, own_keys, q_v, out_v, lengths, cap, top, acc, squares, sums, sums_in, gain_v, wide_gain_v, inverse_v,
+    kv_sem, q_sem, len_sem, gain_sem, out_sem,
     recv_sem, fwd_sem, relay_sem, tp_send, tp_recv,
 ):
     rows = query_ref.shape[0]
@@ -41,9 +41,8 @@
 
     def own_kv(g, which):
         src = (keys_ref, values_ref)[which]
-        return pltpu.make_async_copy(
-            src.at[:, columns(g, HEAD_SIZE)], kv.at[0, g, which], kv_sem.at[which, g]
-        )
+        dst = (own_keys.at[g], kv.at[0, g, 1])[which]
+        return pltpu.make_async_copy(src.at[:, columns(g, HEAD_SIZE)], dst, kv_sem.at[which, g])
 
     def own_q(g):
         return pltpu.make_async_copy(query_ref.at[:, columns(g, wide)], q_v.at[g], q_sem.at[g])
@@ -52,6 +51,8 @@
         return pltpu.make_async_copy(out_v.at[g], context_ref.at[:, columns(g, wide)], out_sem.at[g])
 
     own_lengths = pltpu.make_async_copy(lengths_ref, lengths, len_sem)
+    own_gain = pltpu.make_async_copy(gain_ref, gain_v, gain_sem.at[0])
+    give_gain = pltpu.make_async_copy(wide_gain_v, wide_gain_ref, gain_sem.at[1])
 
     for g in range(groups):
         own_kv(g, 0).start()
@@ -59,6 +60,7 @@
     own_lengths.start()
     for g in range(groups):
         own_q(g).start()
+    own_gain.start()
 
     barrier = pltpu.get_barrier_semaphore()
 
@@ -113,6 +115,12 @@
 
     has_last = jnp.minimum(chip, 1)
     greeted = tp_size + has_next + has_last + core * has_next + (1 - core) * has_last
+
+    for g in range(groups):
+        own_kv(g, 0).wait()
+        kv[0, g, 0] = own_keys[g].T
+        own_kv(g, 1).wait()
+
     pl.semaphore_wait(barrier, greeted)
 
     def send(src_slot, dst_slot, g, send_sem, ctx):
@@ -152,60 +160,68 @@
         copy.wait_send()
 
     def pass_on(g, carry):
-        own_kv(g, 0).wait()
-        own_kv(g, 1).wait()
         sends(0, g, start)
         return carry
 
     lax.fori_loop(0, groups, pass_on, 0)
 
     squares[...] = jnp.zeros_like(squares)
+    own_gain.wait()
+    wide_gain_v[...] = gain_v[...].astype(jnp.float32)
+    give_gain.start()
 
     def attend(j, g):
-        k = jnp.concatenate([kv[2 * j, g, 0], kv[2 * j + 1, g, 0]], axis=0)
+        k = jnp.concatenate([kv[2 * j, g, 0], kv[2 * j + 1, g, 0]], axis=1)
         v = jnp.concatenate([kv[2 * j, g, 1], kv[2 * j + 1, g, 1]], axis=0)
         v = jnp.concatenate([v, jnp.ones_like(v)], axis=1)
+        first_head = g * ratio
+
+        def scores(u):
+            q = jnp.concatenate(
+                [q_v[g, :, h * HEAD_SIZE:(h + 1) * HEAD_SIZE] for h in range(u, u + UNIT)], axis=0
+            )
+            return jnp.dot(q, k, preferred_element_type=jnp.float32)
+
+        square = None
+        following = scores(0)
         for u in range(0, ratio, UNIT):
-            heads = range(u, u + UNIT)
-            q = jnp.concatenate(
-                [q_v[g, :, h * HEAD_SIZE:(h + 1) * HEAD_SIZE] for h in heads], axis=0
-            )
-            s = lax.dot_general(
-                q, k, (((1,), (1,)), ((), ())), preferred_element_type=jnp.float32
-            )
-            probs, tops, olds = [], [], []
-            for n, h in enumerate(heads):
+            s = following
+            if u + UNIT < ratio:
+                following = scores(u + UNIT)
+            olds, held = [], []
+            if j > 0:
+                olds = [top[first_head + u + n] for n in range(UNIT)]
+                held = [acc[first_head + u + n] for n in range(UNIT)]
+            probs, tops = [], []
+            for n in range(UNIT):
                 part = jnp.minimum(s[n * rows:(n + 1) * rows], cap[j])
                 high = jnp.broadcast_to(
                     jnp.max(part, axis=1, keepdims=True), (rows, HEAD_SIZE)
                 )
                 if j > 0:
-                    old = top[g * ratio + h]
-                    high = jnp.maximum(old, high)
-                    olds.append(old)
+                    high = jnp.maximum(olds[n], high)
                 tops.append(high)
                 both = jnp.concatenate([high, high], axis=1)
                 probs.append(jnp.exp2((part - both) * factor).astype(jnp.bfloat16))
             update = jnp.dot(
                 jnp.concatenate(probs, axis=0), v, preferred_element_type=jnp.float32
             )
-            for n, h in enumerate(heads):
-                at = g * ratio + h
-                a = update[n * rows:(n + 1) * rows, :HEAD_SIZE]
-                t = update[n * rows:(n + 1) * rows, HEAD_SIZE:]
+            for n in range(UNIT):
+                at = update[n * rows:(n + 1) * rows]
                 if j > 0:
                     correct = jnp.exp2((olds[n] - tops[n]) * factor)
-                    a = a + acc[at, :, :HEAD_SIZE] * correct
-                    t = t + acc[at, :, HEAD_SIZE:] * correct
+                    at = at + held[n] * jnp.concatenate([correct, correct], axis=1)
+                h = u + n
                 if j < pairs - 1:
-                    top[at] = tops[n]
-                    acc[at, :, :HEAD_SIZE] = a
-                    acc[at, :, HEAD_SIZE:] = t
+                    top[first_head + h] = tops[n]
+                    acc[first_head + h] = at
                 else:
-                    c = (a / t).astype(jnp.bfloat16)
+                    c = (at[:, :HEAD_SIZE] / at[:, HEAD_SIZE:]).astype(jnp.bfloat16)
                     out_v[g, :, h * HEAD_SIZE:(h + 1) * HEAD_SIZE] = c
                     c = c.astype(jnp.float32)
-                    squares[...] += c * c
+                    square = c * c if square is None else square + c * c
+        if square is not None:
+            squares[...] += square
 
     for j in range(pairs):
         def step(g, carry):
@@ -258,7 +274,11 @@
         total = total + sums_in[o, 0:1, :]
     power = total / (QUERY_HEADS * HEAD_SIZE)
     inverse = 1.0 / jnp.sqrt(power + 1e-06)
-    inverse_ref[...] = jnp.broadcast_to(inverse, (rows, rows)).T
+    inverse_v[...] = jnp.broadcast_to(inverse, (rows, rows)).T
+    give_inverse = pltpu.make_async_copy(inverse_v, inverse_ref, len_sem)
+    give_inverse.start()
+    give_gain.wait()
+    give_inverse.wait()
 
 
 def body(ctx_size, tp_size, query, keys, values, doc_lengths, gain):
@@ -269,19 +289,23 @@
     longest = rows * ctx_size * 5 // 8
     back = min(-(-(longest - 1) // rows), ctx_size - 1)
     pairs = back // 2 + 1
-    context, inverse = pl.pallas_call(
+    gain_rows = gain.shape[0] // HEAD_SIZE
+    context, inverse, wide_gain = pl.pallas_call(
         functools.partial(attention_kernel, ctx_size, tp_size, back, ratio),
         out_shape=(
-            jax.ShapeDtypeStruct(query.shape, jnp.bfloat16),
-            jax.ShapeDtypeStruct((rows, rows), jnp.float32),
-        ),
-        in_specs=[pl.BlockSpec(memory_space=pltpu.HBM)] * 4,
+            pltpu.VMEM(query.shape, jnp.bfloat16),
+            pltpu.VMEM((rows, rows), jnp.float32),
+            pltpu.VMEM((gain_rows, HEAD_SIZE), jnp.float32),
+        ),
+        in_specs=[pl.BlockSpec(memory_space=pltpu.HBM)] * 5,
         out_specs=(
             pl.BlockSpec(memory_space=pl.ANY),
-            pl.BlockSpec(memory_space=pltpu.VMEM),
+            pl.BlockSpec(memory_space=pl.ANY),
+            pl.BlockSpec(memory_space=pl.ANY),
         ),
         scratch_shapes=[
             pltpu.VMEM((2 * pairs, groups, 2, rows, HEAD_SIZE), jnp.bfloat16),
+            pltpu.VMEM((groups, rows, HEAD_SIZE), jnp.bfloat16),
             pltpu.VMEM((groups, rows, ratio * HEAD_SIZE), jnp.bfloat16),
             pltpu.VMEM((groups, rows, ratio * HEAD_SIZE), jnp.bfloat16),
             pltpu.SMEM(doc_lengths.shape, jnp.int32),
@@ -291,9 +315,13 @@
             pltpu.VMEM((rows, HEAD_SIZE), jnp.float32),
             pltpu.VMEM((8, rows), jnp.float32),
             pltpu.VMEM((tp_size, 8, rows), jnp.float32),
+            pltpu.VMEM((gain_rows, HEAD_SIZE), jnp.bfloat16),
+            pltpu.VMEM((gain_rows, HEAD_SIZE), jnp.float32),
+            pltpu.VMEM((rows, rows), jnp.float32),
             pltpu.SemaphoreType.DMA((2, groups)),
             pltpu.SemaphoreType.DMA((groups,)),
             pltpu.SemaphoreType.DMA,
+            pltpu.SemaphoreType.DMA((2,)),
             pltpu.SemaphoreType.DMA((groups,)),
             pltpu.SemaphoreType.DMA((2 * pairs, groups)),
             pltpu.SemaphoreType.DMA((pairs, groups)),
@@ -302,16 +330,16 @@
             pltpu.SemaphoreType.DMA((tp_size,)),
         ],
         compiler_params=pltpu.CompilerParams(
-            collective_id=0, has_side_effects=True, vmem_limit_bytes=40 * 2**20
+            collective_id=0, has_side_effects=True, vmem_limit_bytes=56 * 2**20
         ),
         cost_estimate=pl.CostEstimate(
             flops=4 * heads * rows * 2 * pairs * rows * HEAD_SIZE,
             bytes_accessed=4 * query.size + 4 * keys.size,
             transcendentals=heads * rows * 2 * pairs * rows,
         ),
-    )(query, keys, values, doc_lengths)
+    )(query, keys, values, doc_lengths, gain.reshape(gain_rows, HEAD_SIZE))
     return (
-        context.astype(jnp.float32) * gain.astype(jnp.float32)[None, :] * inverse[:, :1]
+        context.astype(jnp.float32) * wide_gain.reshape(1, -1) * inverse[:, :1]
     ).astype(jnp.bfloat16)
 
 

time: 30 us -> 24.9 us (0.83)
  local copies, waits for them, and re-layouts: 3.97 us -> 0.1 us
  other arithmetic: 2.28 us -> 1.57 us
  Pallas kernels: 23.5 us -> 23.1 us
    unnamed x8 -> x0, local copies, waits for them, and re-layouts: 3.87 us -> none
    convert_element_type x2 -> x1, other arithmetic: 2.28 us -> 1.57 us  [body(): return (context.astype(jnp.float32) * wide_gain.reshape(1, -1) * inverse[...]
    pallas_call x1, Pallas kernels: 23.5 us -> 23.1 us  [body(): pl.pallas_call(functools.partial(attention_kernel, ctx_size, tp_size, bac...]
where the time goes in v2:
time: 24.9 us; the launch traced here: 24.7 us
  Pallas kernels  23.1 us (93%)
  other arithmetic  1.57 us (6%)
    pallas_call x1, Pallas kernels, body(): pl.pallas_call(functools.partial(attention_kernel, ctx_size, tp_size, bac...  23.1 us
    convert_element_type x1, other arithmetic, body(): return (context.astype(jnp.float32) * wide_gain.reshape(1, -1) * inverse[...  1.57 us

profile of v2, /device:TPU:24, one launch (start us, length us, event | category | flops | bytes accessed | tf_op | source)
XLA Modules:
  0.0 24.7 jit_solution(18023794539419043014)
XLA Ops:
  0.0 23.1 %shard_map.55 = (bf16[128,6144]{1,0:T(8,128)(2,1)S(1)}, f32[128,128]{1,0:T(8,128)S(1)}, f32[48,128]{1,0:T(8,128)S(1)}) custom-call(bf16[128,6144]{1,0:T(8,128)(2,1)} %query_ref.1, bf16[128,512]{1,0:T(8,128)(2,1)} %keys_ref.1, bf16[128,512]{1,0:T(8,128)(2,1)} %values_ref.1, s32[16]{0:T(128)} %lengths_ref.1, bf16[48,128]{1,0:T(8,128)(2,1)} %bitcast.3), custom_call_target="tpu_custom_call" | custom-call | flops 2415919104 | bytes 3407872 | tf_op jit(solution)/shard_map/pallas_call | solution.py:293
  23.1 0.1 slice_reduce_fusion
  23.2 1.6 %multiply_convert_fusion = bf16[128,6144]{1,0:T(8,128)(2,1)} fusion(bf16[128,6144]{1,0:T(8,128)(2,1)S(1)} %get-tuple-element.8, f32[128]{0:T(128)S(1)} %slice_reduce_fusion, f32[6144]{0:T(1024)S(1)} %bitcast.2), kind=kLoop, calls=%fused_computation | loop fusion | flops 3145728 | bytes 3170816 | tf_op jit(solution)/shard_map/convert_element_type | solution.py:343

commit v3 on v2

--- a/solution.py
+++ b/solution.py
@@ -12,14 +12,16 @@
 HEAD_SIZE = 128
 LOW = -1e31
 MESH = pl.DeviceIdType.MESH
-UNIT = 4
+UNIT = 2
+ONES = 16
+AHEAD = 2
 
 
 def attention_kernel(
     ctx_size, tp_size, back, ratio,
     query_ref, keys_ref, values_ref, lengths_ref, gain_ref,
     context_ref, inverse_ref, wide_gain_ref,
-    kv, own_keys, q_v, out_v, lengths, cap, top, acc, squares, sums, sums_in, gain_v, wide_gain_v, inverse_v,
+    kv, own_values, q_v, q_t, out_v, lengths, cap, top, acc, squares, sums, sums_in, gain_v, wide_gain_v, inverse_v,
     kv_sem, q_sem, len_sem, gain_sem, out_sem,
     recv_sem, fwd_sem, relay_sem, tp_send, tp_recv,
 ):
@@ -41,7 +43,7 @@
 
     def own_kv(g, which):
         src = (keys_ref, values_ref)[which]
-        dst = (own_keys.at[g], kv.at[0, g, 1])[which]
+        dst = (kv.at[0, g, 0], own_values.at[g])[which]
         return pltpu.make_async_copy(src.at[:, columns(g, HEAD_SIZE)], dst, kv_sem.at[which, g])
 
     def own_q(g):
@@ -99,17 +101,17 @@
             pl.when(me < d)(clear)
 
     own_lengths.wait()
-    position = me * rows + lax.broadcasted_iota(jnp.int32, (rows, rows), 0)
-    lane = lax.broadcasted_iota(jnp.int32, (rows, rows), 1)
+    position = me * rows + lax.broadcasted_iota(jnp.int32, (rows, rows), 1)
+    offset = lax.broadcasted_iota(jnp.int32, (rows, rows), 0)
     first = jnp.zeros((rows, rows), jnp.int32)
     end = jnp.int32(0)
     for i in range(docs):
         end = end + lengths[i]
         first = jnp.where(position >= end, end, first)
     for d in range(2 * pairs):
-        key = (me - d) * rows + lane
+        key = (me - d) * rows + offset
         allowed = (key >= first) & (key <= position)
-        cap[d // 2, :, (d % 2) * rows:(d % 2 + 1) * rows] = jnp.where(
+        cap[d // 2, (d % 2) * rows:(d % 2 + 1) * rows, :] = jnp.where(
             allowed, jnp.float32(jnp.inf), jnp.float32(LOW)
         )
 
@@ -117,41 +119,47 @@
     greeted = tp_size + has_next + has_last + core * has_next + (1 - core) * has_last
 
     for g in range(groups):
+        own_kv(g, 1).wait()
+        kv[0, g, 1] = own_values[g].T
         own_kv(g, 0).wait()
-        kv[0, g, 0] = own_keys[g].T
-        own_kv(g, 1).wait()
 
     pl.semaphore_wait(barrier, greeted)
 
-    def send(src_slot, dst_slot, g, send_sem, ctx):
+    def send(half, src_slot, dst_slot, g, send_sem, ctx):
         return pltpu.make_async_remote_copy(
             src_ref=kv.at[src_slot, g],
             dst_ref=kv.at[dst_slot, g],
-            send_sem=send_sem.at[src_slot // 2, g],
+            send_sem=send_sem.at[half, g],
             recv_sem=recv_sem.at[dst_slot, g],
             device_id={"ctx": ctx},
             device_id_type=MESH,
         )
 
     def arrived(d, g):
-        send(0, d, g, fwd_sem, me + 1 - 2 * core).wait_recv()
-
-    def sends(e, g, act):
-        if e + 2 <= back:
-            @pl.when(has_next == 1)
+        send(0, 0, d, g, fwd_sem, me + 1 - 2 * core).wait_recv()
+
+    def forward(n, act):
+        half, g = n // groups, lax.rem(n, groups)
+        e = 2 * half
+        held = jnp.minimum(jnp.maximum(me - e + 1, 0), 1) * has_next
+
+        @pl.when(held * jnp.minimum(jnp.maximum(back - e - 1, 0), 1) == 1)
+        def _():
+            act(send(half, e, e + 2, g, fwd_sem, me + 2))
+
+        if back % 2 == 1:
+            @pl.when((held * core == 1) & (e + 1 == back))
             def _():
-                act(send(e, e + 2, g, fwd_sem, me + 2))
+                act(send(half, e, e + 1, g, fwd_sem, me + 1))
+
+    def relay(e, g, act):
+        copy = send(e // 2, e, e + 1 - 2 * core, g, relay_sem, me + 1 - 2 * core)
+        if e == 0:
+            pl.when(core == 0)(lambda: act(copy))
         elif e + 1 <= back:
-            @pl.when(core * has_next == 1)
-            def _():
-                act(send(e, e + 1, g, fwd_sem, me + 1))
-        relay = send(e, e + 1 - 2 * core, g, relay_sem, me + 1 - 2 * core)
-        if e == 0:
-            pl.when(core == 0)(lambda: act(relay))
-        elif e + 1 <= back:
-            act(relay)
+            act(copy)
         else:
-            pl.when(core == 1)(lambda: act(relay))
+            pl.when(core == 1)(lambda: act(copy))
 
     def start(copy):
         copy.start()
@@ -159,11 +167,23 @@
     def finish(copy):
         copy.wait_send()
 
+    for n in range(AHEAD):
+        forward(jnp.int32(n), start)
+
     def pass_on(g, carry):
-        sends(0, g, start)
+        relay(0, g, start)
         return carry
 
     lax.fori_loop(0, groups, pass_on, 0)
+
+    def turn(g, carry):
+        own_q(g).wait()
+        for h in range(ratio):
+            at = slice(h * HEAD_SIZE, (h + 1) * HEAD_SIZE)
+            q_t[g, :, h * rows:(h + 1) * rows] = q_v[g, :, at].T
+        return carry
+
+    lax.fori_loop(0, groups, turn, 0)
 
     squares[...] = jnp.zeros_like(squares)
     own_gain.wait()
@@ -171,16 +191,14 @@
     give_gain.start()
 
     def attend(j, g):
-        k = jnp.concatenate([kv[2 * j, g, 0], kv[2 * j + 1, g, 0]], axis=1)
-        v = jnp.concatenate([kv[2 * j, g, 1], kv[2 * j + 1, g, 1]], axis=0)
-        v = jnp.concatenate([v, jnp.ones_like(v)], axis=1)
+        k = jnp.concatenate([kv[2 * j, g, 0], kv[2 * j + 1, g, 0]], axis=0)
+        v = jnp.concatenate([kv[2 * j, g, 1], kv[2 * j + 1, g, 1]], axis=1)
+        v = jnp.concatenate([v, jnp.ones((ONES, 2 * rows), v.dtype)], axis=0)
         first_head = g * ratio
 
         def scores(u):
-            q = jnp.concatenate(
-                [q_v[g, :, h * HEAD_SIZE:(h + 1) * HEAD_SIZE] for h in range(u, u + UNIT)], axis=0
-            )
-            return jnp.dot(q, k, preferred_element_type=jnp.float32)
+            q = q_t[g, :, u * rows:(u + UNIT) * rows]
+            return jnp.dot(k, q, preferred_element_type=jnp.float32)
 
         square = None
         following = scores(0)
@@ -194,30 +212,27 @@
                 held = [acc[first_head + u + n] for n in range(UNIT)]
             probs, tops = [], []
             for n in range(UNIT):
-                part = jnp.minimum(s[n * rows:(n + 1) * rows], cap[j])
-                high = jnp.broadcast_to(
-                    jnp.max(part, axis=1, keepdims=True), (rows, HEAD_SIZE)
-                )
+                part = jnp.minimum(s[:, n * rows:(n + 1) * rows], cap[j])
+                high = jnp.max(part, axis=0, keepdims=True)
                 if j > 0:
                     high = jnp.maximum(olds[n], high)
                 tops.append(high)
-                both = jnp.concatenate([high, high], axis=1)
-                probs.append(jnp.exp2((part - both) * factor).astype(jnp.bfloat16))
+                probs.append(jnp.exp2((part - high) * factor).astype(jnp.bfloat16))
             update = jnp.dot(
-                jnp.concatenate(probs, axis=0), v, preferred_element_type=jnp.float32
+                v, jnp.concatenate(probs, axis=1), preferred_element_type=jnp.float32
             )
             for n in range(UNIT):
-                at = update[n * rows:(n + 1) * rows]
+                at = update[:, n * rows:(n + 1) * rows]
                 if j > 0:
-                    correct = jnp.exp2((olds[n] - tops[n]) * factor)
-                    at = at + held[n] * jnp.concatenate([correct, correct], axis=1)
+                    at = at + held[n] * jnp.exp2((olds[n] - tops[n]) * factor)
                 h = u + n
                 if j < pairs - 1:
                     top[first_head + h] = tops[n]
                     acc[first_head + h] = at
                 else:
-                    c = (at[:, :HEAD_SIZE] / at[:, HEAD_SIZE:]).astype(jnp.bfloat16)
-                    out_v[g, :, h * HEAD_SIZE:(h + 1) * HEAD_SIZE] = c
+                    share = 1.0 / at[HEAD_SIZE:HEAD_SIZE + 1]
+                    c = (at[:HEAD_SIZE] * share).astype(jnp.bfloat16)
+                    out_v[g, :, h * HEAD_SIZE:(h + 1) * HEAD_SIZE] = c.T
                     c = c.astype(jnp.float32)
                     square = c * c if square is None else square + c * c
         if square is not None:
@@ -230,13 +245,18 @@
                 @pl.when(me >= even)
                 def _():
                     arrived(even, g)
-                    sends(even, g, start)
+                    relay(even, g, start)
+            n = j * groups + g
+
+            @pl.when(n + AHEAD < pairs * groups)
+            def _():
+                forward(n, finish)
+                forward(n + AHEAD, start)
+
             if odd <= back:
                 @pl.when(me >= odd)
                 def _():
                     arrived(odd, g)
-            if j == 0:
-                own_q(g).wait()
             attend(j, g)
             if j == pairs - 1:
                 write_out(g).start()
@@ -244,7 +264,7 @@
 
         lax.fori_loop(0, groups, step, 0)
 
-    mine = jnp.sum(squares[...].T, axis=0, keepdims=True)
+    mine = jnp.sum(squares[...], axis=0, keepdims=True)
     sums[...] = jnp.broadcast_to(mine, sums.shape)
     copies = []
     for o in range(1, tp_size):
@@ -261,13 +281,15 @@
     def drain(g, carry):
         for e in range(0, back + 1, 2):
             if e == 0:
-                sends(e, g, finish)
+                relay(e, g, finish)
             else:
-                pl.when(me >= e)(lambda: sends(e, g, finish))
+                pl.when(me >= e)(lambda: relay(e, g, finish))
         write_out(g).wait()
         return carry
 
     lax.fori_loop(0, groups, drain, 0)
+    for n in range(pairs * groups - AHEAD, pairs * groups):
+        forward(jnp.int32(n), finish)
     total = mine
     for o, copy in enumerate(copies):
         copy.wait()
@@ -307,12 +329,13 @@
             pltpu.VMEM((2 * pairs, groups, 2, rows, HEAD_SIZE), jnp.bfloat16),
             pltpu.VMEM((groups, rows, HEAD_SIZE), jnp.bfloat16),
             pltpu.VMEM((groups, rows, ratio * HEAD_SIZE), jnp.bfloat16),
+            pltpu.VMEM((groups, HEAD_SIZE, ratio * rows), jnp.bfloat16),
             pltpu.VMEM((groups, rows, ratio * HEAD_SIZE), jnp.bfloat16),
             pltpu.SMEM(doc_lengths.shape, jnp.int32),
-            pltpu.VMEM((pairs, rows, 2 * rows), jnp.float32),
-            pltpu.VMEM((heads, rows, HEAD_SIZE), jnp.float32),
-            pltpu.VMEM((heads, rows, 2 * HEAD_SIZE), jnp.float32),
-            pltpu.VMEM((rows, HEAD_SIZE), jnp.float32),
+            pltpu.VMEM((pairs, 2 * rows, rows), jnp.float32),
+            pltpu.VMEM((heads, 1, rows), jnp.float32),
+            pltpu.VMEM((heads, HEAD_SIZE + ONES, rows), jnp.float32),
+            pltpu.VMEM((HEAD_SIZE, rows), jnp.float32),
             pltpu.VMEM((8, rows), jnp.float32),
             pltpu.VMEM((tp_size, 8, rows), jnp.float32),
             pltpu.VMEM((gain_rows, HEAD_SIZE), jnp.bfloat16),

time: 24.9 us -> 26.2 us (1.052)
  Pallas kernels: 23.1 us -> 24.4 us
    pallas_call x1, Pallas kernels: 23.1 us -> 24.4 us  [body(): pl.pallas_call(functools.partial(attention_kernel, ctx_size, tp_size, bac...]
where the time goes in v3:
time: 26.2 us; the launch traced here: 26.1 us
  Pallas kernels  24.4 us (93%)
  other arithmetic  1.57 us (6%)
    pallas_call x1, Pallas kernels, body(): pl.pallas_call(functools.partial(attention_kernel, ctx_size, tp_size, bac...  24.4 us
    convert_element_type x1, other arithmetic, body(): return (context.astype(jnp.float32) * wide_gain.reshape(1, -1) * inverse[...  1.57 us

profile of v3, /device:TPU:24, one launch (start us, length us, event | category | flops | bytes accessed | tf_op | source)
XLA Modules:
  0.0 26.1 jit_solution(820056082353016741)
XLA Ops:
  0.0 24.4 %shard_map.55 = (bf16[128,6144]{1,0:T(8,128)(2,1)S(1)}, f32[128,128]{1,0:T(8,128)S(1)}, f32[48,128]{1,0:T(8,128)S(1)}) custom-call(bf16[128,6144]{1,0:T(8,128)(2,1)} %query_ref.1, bf16[128,512]{1,0:T(8,128)(2,1)} %keys_ref.1, bf16[128,512]{1,0:T(8,128)(2,1)} %values_ref.1, s32[16]{0:T(128)} %lengths_ref.1, bf16[48,128]{1,0:T(8,128)(2,1)} %bitcast.3), custom_call_target="tpu_custom_call" | custom-call | flops 2415919104 | bytes 3407872 | tf_op jit(solution)/shard_map/pallas_call | solution.py:315
  24.4 0.1 slice_reduce_fusion
  24.5 1.6 %multiply_convert_fusion = bf16[128,6144]{1,0:T(8,128)(2,1)} fusion(bf16[128,6144]{1,0:T(8,128)(2,1)S(1)} %get-tuple-element.8, f32[128]{0:T(128)S(1)} %slice_reduce_fusion, f32[6144]{0:T(1024)S(1)} %bitcast.2), kind=kLoop, calls=%fused_computation | loop fusion | flops 3145728 | bytes 3170816 | tf_op jit(solution)/shard_map/convert_element_type | solution.py:366

commit v4 on v2

--- a/solution.py
+++ b/solution.py
@@ -13,6 +13,7 @@
 LOW = -1e31
 MESH = pl.DeviceIdType.MESH
 UNIT = 4
+AHEAD = 2
 
 
 def attention_kernel(
@@ -26,7 +27,8 @@
     rows = query_ref.shape[0]
     groups = keys_ref.shape[1] // HEAD_SIZE
     wide = ratio * HEAD_SIZE
-    pairs = back // 2 + 1
+    steps = [[0]] + [list(range(d, min(d + 2, back + 1))) for d in range(1, back + 1, 2)]
+    chunks = (len(steps) - 1) * groups
     docs = lengths.shape[0]
     chips = ctx_size // 2
     me = lax.axis_index("ctx")
@@ -90,26 +92,23 @@
             barrier, inc=1, device_id={"tp": lax.rem(my_tp + o, tp_size)}, device_id_type=MESH
         )
 
-    for d in range(1, 2 * pairs):
+    for d in range(1, back + 1):
         def clear():
             kv[d] = jnp.zeros_like(kv[d])
-        if d > back:
-            clear()
-        else:
-            pl.when(me < d)(clear)
+        pl.when(me < d)(clear)
 
     own_lengths.wait()
     position = me * rows + lax.broadcasted_iota(jnp.int32, (rows, rows), 0)
-    lane = lax.broadcasted_iota(jnp.int32, (rows, rows), 1)
+    offset = lax.broadcasted_iota(jnp.int32, (rows, rows), 1)
     first = jnp.zeros((rows, rows), jnp.int32)
     end = jnp.int32(0)
     for i in range(docs):
         end = end + lengths[i]
         first = jnp.where(position >= end, end, first)
-    for d in range(2 * pairs):
-        key = (me - d) * rows + lane
+    for d in range(back + 1):
+        key = (me - d) * rows + offset
         allowed = (key >= first) & (key <= position)
-        cap[d // 2, :, (d % 2) * rows:(d % 2 + 1) * rows] = jnp.where(
+        cap[d] = jnp.where(
             allowed, jnp.float32(jnp.inf), jnp.float32(LOW)
         )
 
@@ -123,35 +122,41 @@
 
     pl.semaphore_wait(barrier, greeted)
 
-    def send(src_slot, dst_slot, g, send_sem, ctx):
+    def send(half, src_slot, dst_slot, g, send_sem, ctx):
         return pltpu.make_async_remote_copy(
             src_ref=kv.at[src_slot, g],
             dst_ref=kv.at[dst_slot, g],
-            send_sem=send_sem.at[src_slot // 2, g],
+            send_sem=send_sem.at[half, g],
             recv_sem=recv_sem.at[dst_slot, g],
             device_id={"ctx": ctx},
             device_id_type=MESH,
         )
 
     def arrived(d, g):
-        send(0, d, g, fwd_sem, me + 1 - 2 * core).wait_recv()
-
-    def sends(e, g, act):
-        if e + 2 <= back:
-            @pl.when(has_next == 1)
+        send(0, 0, d, g, fwd_sem, me + 1 - 2 * core).wait_recv()
+
+    def forward(n, act):
+        half, g = n // groups, lax.rem(n, groups)
+        e = 2 * half
+        held = jnp.minimum(jnp.maximum(me - e + 1, 0), 1) * has_next
+
+        @pl.when(held * jnp.minimum(jnp.maximum(back - e - 1, 0), 1) == 1)
+        def _():
+            act(send(half, e, e + 2, g, fwd_sem, me + 2))
+
+        if back % 2 == 1:
+            @pl.when((held * core == 1) & (e + 1 == back))
             def _():
-                act(send(e, e + 2, g, fwd_sem, me + 2))
+                act(send(half, e, e + 1, g, fwd_sem, me + 1))
+
+    def relay(e, g, act):
+        copy = send(e // 2, e, e + 1 - 2 * core, g, relay_sem, me + 1 - 2 * core)
+        if e == 0:
+            pl.when(core == 0)(lambda: act(copy))
         elif e + 1 <= back:
-            @pl.when(core * has_next == 1)
-            def _():
-                act(send(e, e + 1, g, fwd_sem, me + 1))
-        relay = send(e, e + 1 - 2 * core, g, relay_sem, me + 1 - 2 * core)
-        if e == 0:
-            pl.when(core == 0)(lambda: act(relay))
-        elif e + 1 <= back:
-            act(relay)
+            act(copy)
         else:
-            pl.when(core == 1)(lambda: act(relay))
+            pl.when(core == 1)(lambda: act(copy))
 
     def start(copy):
         copy.start()
@@ -159,8 +164,11 @@
     def finish(copy):
         copy.wait_send()
 
+    for n in range(AHEAD):
+        forward(jnp.int32(n), start)
+
     def pass_on(g, carry):
-        sends(0, g, start)
+        relay(0, g, start)
         return carry
 
     lax.fori_loop(0, groups, pass_on, 0)
@@ -171,9 +179,11 @@
     give_gain.start()
 
     def attend(j, g):
-        k = jnp.concatenate([kv[2 * j, g, 0], kv[2 * j + 1, g, 0]], axis=1)
-        v = jnp.concatenate([kv[2 * j, g, 1], kv[2 * j + 1, g, 1]], axis=0)
+        slots = steps[j]
+        k = jnp.concatenate([kv[d, g, 0] for d in slots], axis=1)
+        v = jnp.concatenate([kv[d, g, 1] for d in slots], axis=0)
         v = jnp.concatenate([v, jnp.ones_like(v)], axis=1)
+        limit = jnp.concatenate([cap[d] for d in slots], axis=1)
         first_head = g * ratio
 
         def scores(u):
@@ -194,15 +204,15 @@
                 held = [acc[first_head + u + n] for n in range(UNIT)]
             probs, tops = [], []
             for n in range(UNIT):
-                part = jnp.minimum(s[n * rows:(n + 1) * rows], cap[j])
+                part = jnp.minimum(s[n * rows:(n + 1) * rows], limit)
                 high = jnp.broadcast_to(
                     jnp.max(part, axis=1, keepdims=True), (rows, HEAD_SIZE)
                 )
                 if j > 0:
                     high = jnp.maximum(olds[n], high)
                 tops.append(high)
-                both = jnp.concatenate([high, high], axis=1)
-                probs.append(jnp.exp2((part - both) * factor).astype(jnp.bfloat16))
+                wide_high = jnp.concatenate([high] * len(slots), axis=1)
+                probs.append(jnp.exp2((part - wide_high) * factor).astype(jnp.bfloat16))
             update = jnp.dot(
                 jnp.concatenate(probs, axis=0), v, preferred_element_type=jnp.float32
             )
@@ -212,7 +222,7 @@
                     correct = jnp.exp2((olds[n] - tops[n]) * factor)
                     at = at + held[n] * jnp.concatenate([correct, correct], axis=1)
                 h = u + n
-                if j < pairs - 1:
+                if j < len(steps) - 1:
                     top[first_head + h] = tops[n]
                     acc[first_head + h] = at
                 else:
@@ -223,22 +233,29 @@
         if square is not None:
             squares[...] += square
 
-    for j in range(pairs):
+    for j in range(len(steps)):
         def step(g, carry):
-            even, odd = 2 * j + 2, 2 * j + 1
-            if even <= back:
-                @pl.when(me >= even)
+            if j == 0:
+                own_q(g).wait()
+            else:
+                odd, even = 2 * j - 1, 2 * j
+                if even <= back:
+                    @pl.when(me >= even)
+                    def _():
+                        arrived(even, g)
+                        relay(even, g, start)
+                n = (j - 1) * groups + g
+
+                @pl.when(n + AHEAD < chunks)
                 def _():
-                    arrived(even, g)
-                    sends(even, g, start)
-            if odd <= back:
+                    forward(n, finish)
+                    forward(n + AHEAD, start)
+
                 @pl.when(me >= odd)
                 def _():
                     arrived(odd, g)
-            if j == 0:
-                own_q(g).wait()
             attend(j, g)
-            if j == pairs - 1:
+            if j == len(steps) - 1:
                 write_out(g).start()
             return carry
 
@@ -261,13 +278,15 @@
     def drain(g, carry):
         for e in range(0, back + 1, 2):
             if e == 0:
-                sends(e, g, finish)
+                relay(e, g, finish)
             else:
-                pl.when(me >= e)(lambda: sends(e, g, finish))
+                pl.when(me >= e)(lambda: relay(e, g, finish))
         write_out(g).wait()
         return carry
 
     lax.fori_loop(0, groups, drain, 0)
+    for n in range(chunks - AHEAD, chunks):
+        forward(jnp.int32(n), finish)
     total = mine
     for o, copy in enumerate(copies):
         copy.wait()
@@ -288,7 +307,7 @@
     ratio = heads // groups
     longest = rows * ctx_size * 5 // 8
     back = min(-(-(longest - 1) // rows), ctx_size - 1)
-    pairs = back // 2 + 1
+    halves = back // 2 + 1
     gain_rows = gain.shape[0] // HEAD_SIZE
     context, inverse, wide_gain = pl.pallas_call(
         functools.partial(attention_kernel, ctx_size, tp_size, back, ratio),
@@ -304,12 +323,12 @@
             pl.BlockSpec(memory_space=pl.ANY),
         ),
         scratch_shapes=[
-            pltpu.VMEM((2 * pairs, groups, 2, rows, HEAD_SIZE), jnp.bfloat16),
+            pltpu.VMEM((back + 1, groups, 2, rows, HEAD_SIZE), jnp.bfloat16),
             pltpu.VMEM((groups, rows, HEAD_SIZE), jnp.bfloat16),
             pltpu.VMEM((groups, rows, ratio * HEAD_SIZE), jnp.bfloat16),
             pltpu.VMEM((groups, rows, ratio * HEAD_SIZE), jnp.bfloat16),
             pltpu.SMEM(doc_lengths.shape, jnp.int32),
-            pltpu.VMEM((pairs, rows, 2 * rows), jnp.float32),
+            pltpu.VMEM((back + 1, rows, rows), jnp.float32),
             pltpu.VMEM((heads, rows, HEAD_SIZE), jnp.float32),
             pltpu.VMEM((heads, rows, 2 * HEAD_SIZE), jnp.float32),
             pltpu.VMEM((rows, HEAD_SIZE), jnp.float32),
@@ -323,9 +342,9 @@
             pltpu.SemaphoreType.DMA,
             pltpu.SemaphoreType.DMA((2,)),
             pltpu.SemaphoreType.DMA((groups,)),
-            pltpu.SemaphoreType.DMA((2 * pairs, groups)),
-            pltpu.SemaphoreType.DMA((pairs, groups)),
-            pltpu.SemaphoreType.DMA((pairs, groups)),
+            pltpu.SemaphoreType.DMA((back + 1, groups)),
+            pltpu.SemaphoreType.DMA((halves, groups)),
+            pltpu.SemaphoreType.DMA((halves, groups)),
             pltpu.SemaphoreType.DMA((tp_size,)),
             pltpu.SemaphoreType.DMA((tp_size,)),
         ],
@@ -333,9 +352,9 @@
             collective_id=0, has_side_effects=True, vmem_limit_bytes=56 * 2**20
         ),
         cost_estimate=pl.CostEstimate(
-            flops=4 * heads * rows * 2 * pairs * rows * HEAD_SIZE,
+            flops=4 * heads * rows * (back + 1) * rows * HEAD_SIZE,
             bytes_accessed=4 * query.size + 4 * keys.size,
-            transcendentals=heads * rows * 2 * pairs * rows,
+            transcendentals=heads * rows * (back + 1) * rows,
         ),
     )(query, keys, values, doc_lengths, gain.reshape(gain_rows, HEAD_SIZE))
     return (

time: 24.9 us -> 25.2 us (1.012)
  Pallas kernels: 23.1 us -> 23.4 us
    pallas_call x1, Pallas kernels: 23.1 us -> 23.4 us  [body(): pl.pallas_call(functools.partial(attention_kernel, ctx_size, tp_size, bac...]
where the time goes in v4:
time: 25.2 us; the launch traced here: 25.1 us
  Pallas kernels  23.4 us (93%)
  other arithmetic  1.57 us (6%)
    pallas_call x1, Pallas kernels, body(): pl.pallas_call(functools.partial(attention_kernel, ctx_size, tp_size, bac...  23.4 us
    convert_element_type x1, other arithmetic, body(): return (context.astype(jnp.float32) * wide_gain.reshape(1, -1) * inverse[...  1.57 us

profile of v4, /device:TPU:24, one launch (start us, length us, event | category | flops | bytes accessed | tf_op | source)
XLA Modules:
  0.0 25.1 jit_solution(13590068056648235801)
XLA Ops:
  0.0 23.4 %shard_map.55 = (bf16[128,6144]{1,0:T(8,128)(2,1)S(1)}, f32[128,128]{1,0:T(8,128)S(1)}, f32[48,128]{1,0:T(8,128)S(1)}) custom-call(bf16[128,6144]{1,0:T(8,128)(2,1)} %query_ref.1, bf16[128,512]{1,0:T(8,128)(2,1)} %keys_ref.1, bf16[128,512]{1,0:T(8,128)(2,1)} %values_ref.1, s32[16]{0:T(128)} %lengths_ref.1, bf16[48,128]{1,0:T(8,128)(2,1)} %bitcast.3), custom_call_target="tpu_custom_call" | custom-call | flops 2415919104 | bytes 3407872 | tf_op jit(solution)/shard_map/pallas_call | solution.py:312
  23.4 0.1 slice_reduce_fusion
  23.5 1.6 %multiply_convert_fusion = bf16[128,6144]{1,0:T(8,128)(2,1)} fusion(bf16[128,6144]{1,0:T(8,128)(2,1)S(1)} %get-tuple-element.8, f32[128]{0:T(128)S(1)} %slice_reduce_fusion, f32[6144]{0:T(1024)S(1)} %bitcast.2), kind=kLoop, calls=%fused_computation | loop fusion | flops 3145728 | bytes 3170816 | tf_op jit(solution)/shard_map/convert_element_type | solution.py:362

commit v5 on v4

--- a/solution.py
+++ b/solution.py
@@ -12,7 +12,7 @@
 HEAD_SIZE = 128
 LOW = -1e31
 MESH = pl.DeviceIdType.MESH
-UNIT = 4
+UNIT = 12
 AHEAD = 2
 
 
@@ -27,8 +27,8 @@
     rows = query_ref.shape[0]
     groups = keys_ref.shape[1] // HEAD_SIZE
     wide = ratio * HEAD_SIZE
-    steps = [[0]] + [list(range(d, min(d + 2, back + 1))) for d in range(1, back + 1, 2)]
-    chunks = (len(steps) - 1) * groups
+    steps = [list(range(d, min(d + 2, back + 1))) for d in range(0, back + 1, 2)]
+    chunks = (back + 1) // 2 * groups
     docs = lengths.shape[0]
     chips = ctx_size // 2
     me = lax.axis_index("ctx")
@@ -235,25 +235,25 @@
 
     for j in range(len(steps)):
         def step(g, carry):
-            if j == 0:
-                own_q(g).wait()
-            else:
-                odd, even = 2 * j - 1, 2 * j
-                if even <= back:
-                    @pl.when(me >= even)
-                    def _():
-                        arrived(even, g)
-                        relay(even, g, start)
-                n = (j - 1) * groups + g
-
-                @pl.when(n + AHEAD < chunks)
+            even, odd = 2 * j + 2, 2 * j + 1
+            if even <= back:
+                @pl.when(me >= even)
                 def _():
-                    forward(n, finish)
-                    forward(n + AHEAD, start)
-
+                    arrived(even, g)
+                    relay(even, g, start)
+            n = j * groups + g
+
+            @pl.when(n + AHEAD < chunks)
+            def _():
+                forward(n, finish)
+                forward(n + AHEAD, start)
+
+            if odd <= back:
                 @pl.when(me >= odd)
                 def _():
                     arrived(odd, g)
+            if j == 0:
+                own_q(g).wait()
             attend(j, g)
             if j == len(steps) - 1:
                 write_out(g).start()

time: 25.2 us -> 25.7 us (1.020)
  Pallas kernels: 23.4 us -> 23.9 us
    pallas_call x1, Pallas kernels: 23.4 us -> 23.9 us  [body(): pl.pallas_call(functools.partial(attention_kernel, ctx_size, tp_size, bac...]
where the time goes in v5:
time: 25.7 us; the launch traced here: 25.6 us
  Pallas kernels  23.9 us (93%)
  other arithmetic  1.57 us (6%)
    pallas_call x1, Pallas kernels, body(): pl.pallas_call(functools.partial(attention_kernel, ctx_size, tp_size, bac...  23.9 us
    convert_element_type x1, other arithmetic, body(): return (context.astype(jnp.float32) * wide_gain.reshape(1, -1) * inverse[...  1.57 us

profile of v5, /device:TPU:24, one launch (start us, length us, event | category | flops | bytes accessed | tf_op | source)
XLA Modules:
  0.0 25.6 jit_solution(10674820650482883524)
XLA Ops:
  0.0 23.9 %shard_map.55 = (bf16[128,6144]{1,0:T(8,128)(2,1)S(1)}, f32[128,128]{1,0:T(8,128)S(1)}, f32[48,128]{1,0:T(8,128)S(1)}) custom-call(bf16[128,6144]{1,0:T(8,128)(2,1)} %query_ref.1, bf16[128,512]{1,0:T(8,128)(2,1)} %keys_ref.1, bf16[128,512]{1,0:T(8,128)(2,1)} %values_ref.1, s32[16]{0:T(128)} %lengths_ref.1, bf16[48,128]{1,0:T(8,128)(2,1)} %bitcast.3), custom_call_target="tpu_custom_call" | custom-call | flops 2415919104 | bytes 3407872 | tf_op jit(solution)/shard_map/pallas_call | solution.py:312
  23.9 0.1 slice_reduce_fusion
  24.0 1.6 %multiply_convert_fusion = bf16[128,6144]{1,0:T(8,128)(2,1)} fusion(bf16[128,6144]{1,0:T(8,128)(2,1)S(1)} %get-tuple-element.8, f32[128]{0:T(128)S(1)} %slice_reduce_fusion, f32[6144]{0:T(1024)S(1)} %bitcast.2), kind=kLoop, calls=%fused_computation | loop fusion | flops 3145728 | bytes 3170816 | tf_op jit(solution)/shard_map/convert_element_type | solution.py:362

commit v6 on v4

--- a/solution.py
+++ b/solution.py
@@ -13,7 +13,7 @@
 LOW = -1e31
 MESH = pl.DeviceIdType.MESH
 UNIT = 4
-AHEAD = 2
+AHEAD = 3
 
 
 def attention_kernel(
@@ -29,6 +29,7 @@
     wide = ratio * HEAD_SIZE
     steps = [[0]] + [list(range(d, min(d + 2, back + 1))) for d in range(1, back + 1, 2)]
     chunks = (len(steps) - 1) * groups
+    ahead = min(AHEAD, groups)
     docs = lengths.shape[0]
     chips = ctx_size // 2
     me = lax.axis_index("ctx")
@@ -164,7 +165,7 @@
     def finish(copy):
         copy.wait_send()
 
-    for n in range(AHEAD):
+    for n in range(ahead):
         forward(jnp.int32(n), start)
 
     def pass_on(g, carry):
@@ -246,10 +247,10 @@
                         relay(even, g, start)
                 n = (j - 1) * groups + g
 
-                @pl.when(n + AHEAD < chunks)
+                @pl.when(n + ahead < chunks)
                 def _():
                     forward(n, finish)
-                    forward(n + AHEAD, start)
+                    forward(n + ahead, start)
 
                 @pl.when(me >= odd)
                 def _():
@@ -285,7 +286,7 @@
         return carry
 
     lax.fori_loop(0, groups, drain, 0)
-    for n in range(chunks - AHEAD, chunks):
+    for n in range(chunks - ahead, chunks):
         forward(jnp.int32(n), finish)
     total = mine
     for o, copy in enumerate(copies):

time: 25.2 us -> 24.6 us (0.976)
  Pallas kernels: 23.4 us -> 22.7 us
    pallas_call x1, Pallas kernels: 23.4 us -> 22.7 us  [body(): pl.pallas_call(functools.partial(attention_kernel, ctx_size, tp_size, bac...]
where the time goes in v6:
time: 24.6 us; the launch traced here: 24.4 us
  Pallas kernels  22.7 us (92%)
  other arithmetic  1.57 us (6%)
    pallas_call x1, Pallas kernels, body(): pl.pallas_call(functools.partial(attention_kernel, ctx_size, tp_size, bac...  22.7 us
    convert_element_type x1, other arithmetic, body(): return (context.astype(jnp.float32) * wide_gain.reshape(1, -1) * inverse[...  1.57 us

profile of v6, /device:TPU:24, one launch (start us, length us, event | category | flops | bytes accessed | tf_op | source)
XLA Modules:
  0.0 24.4 jit_solution(1009530328740155760)
XLA Ops:
  0.0 22.7 %shard_map.55 = (bf16[128,6144]{1,0:T(8,128)(2,1)S(1)}, f32[128,128]{1,0:T(8,128)S(1)}, f32[48,128]{1,0:T(8,128)S(1)}) custom-call(bf16[128,6144]{1,0:T(8,128)(2,1)} %query_ref.1, bf16[128,512]{1,0:T(8,128)(2,1)} %keys_ref.1, bf16[128,512]{1,0:T(8,128)(2,1)} %values_ref.1, s32[16]{0:T(128)} %lengths_ref.1, bf16[48,128]{1,0:T(8,128)(2,1)} %bitcast.3), custom_call_target="tpu_custom_call" | custom-call | flops 2415919104 | bytes 3407872 | tf_op jit(solution)/shard_map/pallas_call | solution.py:313
  22.7 0.1 slice_reduce_fusion
  22.9 1.6 %multiply_convert_fusion = bf16[128,6144]{1,0:T(8,128)(2,1)} fusion(bf16[128,6144]{1,0:T(8,128)(2,1)S(1)} %get-tuple-element.8, f32[128]{0:T(128)S(1)} %slice_reduce_fusion, f32[6144]{0:T(1024)S(1)} %bitcast.2), kind=kLoop, calls=%fused_computation | loop fusion | flops 3145728 | bytes 3170816 | tf_op jit(solution)/shard_map/convert_element_type | solution.py:363

commit v7 on v5

--- a/solution.py
+++ b/solution.py
@@ -12,8 +12,9 @@
 HEAD_SIZE = 128
 LOW = -1e31
 MESH = pl.DeviceIdType.MESH
-UNIT = 12
-AHEAD = 2
+UNIT = 4
+STEP = 5
+AHEAD = 3
 
 
 def attention_kernel(
@@ -27,8 +28,10 @@
     rows = query_ref.shape[0]
     groups = keys_ref.shape[1] // HEAD_SIZE
     wide = ratio * HEAD_SIZE
-    steps = [list(range(d, min(d + 2, back + 1))) for d in range(0, back + 1, 2)]
-    chunks = (back + 1) // 2 * groups
+    steps = [list(range(d, min(d + STEP, back + 1))) for d in range(0, back + 1, STEP)]
+    phases = (back + 1) // 2
+    chunks = phases * groups
+    ahead = min(AHEAD, groups)
     docs = lengths.shape[0]
     chips = ctx_size // 2
     me = lax.axis_index("ctx")
@@ -164,7 +167,7 @@
     def finish(copy):
         copy.wait_send()
 
-    for n in range(AHEAD):
+    for n in range(ahead):
         forward(jnp.int32(n), start)
 
     def pass_on(g, carry):
@@ -233,33 +236,35 @@
         if square is not None:
             squares[...] += square
 
-    for j in range(len(steps)):
-        def step(g, carry):
-            even, odd = 2 * j + 2, 2 * j + 1
+    for p in range(phases):
+        def phase(g, carry):
+            even = 2 * p + 2
             if even <= back:
                 @pl.when(me >= even)
                 def _():
                     arrived(even, g)
                     relay(even, g, start)
-            n = j * groups + g
-
-            @pl.when(n + AHEAD < chunks)
+            n = p * groups + g
+
+            @pl.when(n + ahead < chunks)
             def _():
                 forward(n, finish)
-                forward(n + AHEAD, start)
-
-            if odd <= back:
-                @pl.when(me >= odd)
-                def _():
-                    arrived(odd, g)
-            if j == 0:
-                own_q(g).wait()
-            attend(j, g)
-            if j == len(steps) - 1:
-                write_out(g).start()
+                forward(n + ahead, start)
+
+            for j, slots in enumerate(steps):
+                if (slots[-1] + 1) // 2 - 1 != p:
+                    continue
+                for d in slots:
+                    if d % 2 == 1:
+                        pl.when(me >= d)(lambda d=d: arrived(d, g))
+                if j == 0:
+                    own_q(g).wait()
+                attend(j, g)
+                if j == len(steps) - 1:
+                    write_out(g).start()
             return carry
 
-        lax.fori_loop(0, groups, step, 0)
+        lax.fori_loop(0, groups, phase, 0)
 
     mine = jnp.sum(squares[...].T, axis=0, keepdims=True)
     sums[...] = jnp.broadcast_to(mine, sums.shape)
@@ -285,7 +290,7 @@
         return carry
 
     lax.fori_loop(0, groups, drain, 0)
-    for n in range(chunks - AHEAD, chunks):
+    for n in range(chunks - ahead, chunks):
         forward(jnp.int32(n), finish)
     total = mine
     for o, copy in enumerate(copies):

time: 25.7 us -> 26.8 us (1.043)
  Pallas kernels: 23.9 us -> 25 us
    pallas_call x1, Pallas kernels: 23.9 us -> 25 us  [body(): pl.pallas_call(functools.partial(attention_kernel, ctx_size, tp_size, bac...]
where the time goes in v7:
time: 26.8 us; the launch traced here: 26.6 us
  Pallas kernels  25 us (93%)
  other arithmetic  1.57 us (6%)
    pallas_call x1, Pallas kernels, body(): pl.pallas_call(functools.partial(attention_kernel, ctx_size, tp_size, bac...  25 us
    convert_element_type x1, other arithmetic, body(): return (context.astype(jnp.float32) * wide_gain.reshape(1, -1) * inverse[...  1.57 us

profile of v7, /device:TPU:24, one launch (start us, length us, event | category | flops | bytes accessed | tf_op | source)
XLA Modules:
  0.0 26.6 jit_solution(8484802767980459395)
XLA Ops:
  0.0 25.0 %shard_map.55 = (bf16[128,6144]{1,0:T(8,128)(2,1)S(1)}, f32[128,128]{1,0:T(8,128)S(1)}, f32[48,128]{1,0:T(8,128)S(1)}) custom-call(bf16[128,6144]{1,0:T(8,128)(2,1)} %query_ref.1, bf16[128,512]{1,0:T(8,128)(2,1)} %keys_ref.1, bf16[128,512]{1,0:T(8,128)(2,1)} %values_ref.1, s32[16]{0:T(128)} %lengths_ref.1, bf16[48,128]{1,0:T(8,128)(2,1)} %bitcast.3), custom_call_target="tpu_custom_call" | custom-call | flops 2415919104 | bytes 3407872 | tf_op jit(solution)/shard_map/pallas_call | solution.py:317
  25.0 0.1 slice_reduce_fusion
  25.1 1.6 %multiply_convert_fusion = bf16[128,6144]{1,0:T(8,128)(2,1)} fusion(bf16[128,6144]{1,0:T(8,128)(2,1)S(1)} %get-tuple-element.8, f32[128]{0:T(128)S(1)} %slice_reduce_fusion, f32[6144]{0:T(1024)S(1)} %bitcast.2), kind=kLoop, calls=%fused_computation | loop fusion | flops 3145728 | bytes 3170816 | tf_op jit(solution)/shard_map/convert_element_type | solution.py:367

commit v8 on v7

--- a/solution.py
+++ b/solution.py
@@ -13,7 +13,7 @@
 LOW = -1e31
 MESH = pl.DeviceIdType.MESH
 UNIT = 4
-STEP = 5
+STEP = 2
 AHEAD = 3
 
 

time: 26.8 us -> 25 us (0.933)
  Pallas kernels: 25 us -> 23.1 us
    pallas_call x1, Pallas kernels: 25 us -> 23.1 us  [body(): pl.pallas_call(functools.partial(attention_kernel, ctx_size, tp_size, bac...]
where the time goes in v8:
time: 25 us; the launch traced here: 24.8 us
  Pallas kernels  23.1 us (92%)
  other arithmetic  1.57 us (6%)
    pallas_call x1, Pallas kernels, body(): pl.pallas_call(functools.partial(attention_kernel, ctx_size, tp_size, bac...  23.1 us
    convert_element_type x1, other arithmetic, body(): return (context.astype(jnp.float32) * wide_gain.reshape(1, -1) * inverse[...  1.57 us

profile of v8, /device:TPU:24, one launch (start us, length us, event | category | flops | bytes accessed | tf_op | source)
XLA Modules:
  0.0 24.8 jit_solution(471909178505532563)
XLA Ops:
  0.0 23.1 %shard_map.55 = (bf16[128,6144]{1,0:T(8,128)(2,1)S(1)}, f32[128,128]{1,0:T(8,128)S(1)}, f32[48,128]{1,0:T(8,128)S(1)}) custom-call(bf16[128,6144]{1,0:T(8,128)(2,1)} %query_ref.1, bf16[128,512]{1,0:T(8,128)(2,1)} %keys_ref.1, bf16[128,512]{1,0:T(8,128)(2,1)} %values_ref.1, s32[16]{0:T(128)} %lengths_ref.1, bf16[48,128]{1,0:T(8,128)(2,1)} %bitcast.3), custom_call_target="tpu_custom_call" | custom-call | flops 2415919104 | bytes 3407872 | tf_op jit(solution)/shard_map/pallas_call | solution.py:317
  23.1 0.1 slice_reduce_fusion
  23.2 1.6 %multiply_convert_fusion = bf16[128,6144]{1,0:T(8,128)(2,1)} fusion(bf16[128,6144]{1,0:T(8,128)(2,1)S(1)} %get-tuple-element.8, f32[128]{0:T(128)S(1)} %slice_reduce_fusion, f32[6144]{0:T(1024)S(1)} %bitcast.2), kind=kLoop, calls=%fused_computation | loop fusion | flops 3145728 | bytes 3170816 | tf_op jit(solution)/shard_map/convert_element_type | solution.py:367
